TPU v7x, 32 devices: a whole 2x2x4 slice. The times are simulated.
32 devices in a mesh: wide: 8 (over z, x), narrow: 4 (over y, core).
Axes of the slice: x: 2, y: 2, z: 4, core: 2. Of those that a mesh axis runs over, the one named last changes fastest.
Arguments:
- embeddings: bfloat16 [16384, 768], P(('wide', 'narrow')), may hold values from -6 to 6
- coarse_ids: int32 [16384, 1], P(('wide', 'narrow')), may hold values from 0 to 7; in each aligned block of 512 rows (0 to 511, 512 to 1023, ...) at most 128 rows name the same one
- fine_ids: int32 [16384], P(('wide', 'narrow')), may hold values from 0 to 2047
- centroids: bfloat16 [16384, 768], P(('wide', 'narrow')), may hold values from -6 to 6
- candidates: int32 [128, 8], P(('wide', 'narrow')), may hold values from 0 to 63, as said below
Outputs:
- new_centroids: bfloat16 [16384, 768], P(('wide', 'narrow'))
- best_score: float32 [16384], P(('wide', 'narrow'))
Inputs may be any that keep to these rules, and one draw needn't show every extreme that they name: `candidates`: counting the 32 entries of the 4 consecutive query blocks of one device, at most 8 lie among the 8 blocks of one coarse cluster, and some coarse cluster holds exactly 8 of every device's entries.
All inputs are finite; a program needn't handle non-finite values.
Results may differ from a plain program's by a relative error of at most 0.0055.
Values may be sent and summed in bfloat16 or wider, within the bound.
A program may use at most 192 MiB of HBM per device.

v0:
```python
import jax
import jax.numpy as jnp
from jax import lax
from jax.sharding import PartitionSpec as P

QROWS = 128
CBLK = 256
K_CAND = 8


def slot_ranks(targets, count):
    table = (targets[:, None] == jnp.arange(count, dtype=jnp.int32)[None, :]).astype(jnp.int32)
    ranks = jnp.cumsum(table, axis=0) - 1
    return jnp.sum(ranks * table, axis=1)


def block_maxima(queries, table, picks):
    total, rows_n, width = queries.shape
    group = total // 8
    turns = total // group

    def one_turn(operands):
        query_part, pick_part = operands
        chosen = jnp.take(table, pick_part, axis=0)
        scores = jnp.einsum("gnd,gcd->gnc", query_part, chosen, preferred_element_type=jnp.float32)
        return jnp.max(scores, axis=2)

    result = lax.map(
        one_turn, (queries.reshape(turns, group, rows_n, width), picks.reshape(turns, group))
    )
    return result.reshape(total, rows_n) * width ** (-0.5)


def local(embeddings, coarse_ids, fine_ids, centroids, candidates):
    wide_count = lax.axis_size("wide")
    narrow_count = lax.axis_size("narrow")
    emb_rows, width = embeddings.shape
    cent_rows = centroids.shape[0]
    group_cents = cent_rows * narrow_count
    row_cap = (2 * emb_rows + wide_count - 1) // wide_count
    targets = coarse_ids[:, 0]
    row_pos = targets * row_cap + slot_ranks(targets, wide_count)
    send_rows = jnp.zeros((wide_count * row_cap, width), jnp.bfloat16).at[row_pos].set(embeddings)
    send_fine = jnp.full((wide_count * row_cap,), -1, jnp.int32).at[row_pos].set(fine_ids)
    recv_rows, recv_fine = (
        lax.all_to_all(
            send_rows.reshape(wide_count, row_cap, width),
            "wide",
            split_axis=0,
            concat_axis=0,
            tiled=True,
        ),
        lax.all_to_all(
            send_fine.reshape(wide_count, row_cap), "wide", split_axis=0, concat_axis=0, tiled=True
        ),
    )
    flat_rows = recv_rows.reshape(-1, width)
    flat_fine = recv_fine.reshape(-1)
    columns = jnp.arange(lax.axis_size("narrow") * cent_rows, dtype=jnp.int32)
    one_hot = (flat_fine[:, None] == columns[None, :]).astype(jnp.bfloat16)
    sums = lax.psum_scatter(
        lax.dot_general(
            one_hot, flat_rows, (((0,), (0,)), ((), ())), preferred_element_type=jnp.float32
        ).astype(jnp.bfloat16),
        "narrow",
        scatter_dimension=0,
        tiled=True,
    ).astype(jnp.float32)
    mixed = centroids.astype(jnp.float32) + sums
    scale_row = lax.rsqrt(jnp.mean(mixed * mixed, axis=1, keepdims=True) + 1e-06)
    new_centroids = (mixed * scale_row).astype(jnp.bfloat16)
    gathered = lax.all_gather(new_centroids, "narrow", axis=0, tiled=True)
    block_count = group_cents // CBLK
    block_table = gathered.reshape(block_count, CBLK, width)
    query_count = emb_rows // QROWS
    requests = query_count * K_CAND
    slot_cap = (2 * requests + wide_count - 1) // wide_count
    slot_total = wide_count * slot_cap
    wanted = candidates.reshape(-1)
    owner_group = wanted // block_count
    local_block = wanted - owner_group * block_count
    req_pos = owner_group * slot_cap + slot_ranks(owner_group, wide_count)
    req_query = jnp.arange(requests, dtype=jnp.int32) // K_CAND
    slot_query = jnp.zeros((slot_total,), jnp.int32).at[req_pos].set(req_query)
    slot_live = jnp.zeros((slot_total,), jnp.bool_).at[req_pos].set(True)
    slot_block = jnp.full((slot_total,), -1, jnp.int32).at[req_pos].set(local_block)
    query_blocks = embeddings.reshape(query_count, QROWS, width)
    send_queries = jnp.where(
        slot_live[:, None, None],
        jnp.take(query_blocks, slot_query, axis=0),
        jnp.zeros((), jnp.bfloat16),
    )
    ids_in = lax.all_to_all(
        slot_block.reshape(wide_count, slot_cap), "wide", split_axis=0, concat_axis=0, tiled=True
    )
    picks = jnp.clip(ids_in.reshape(-1), 0, block_count - 1)
    outgoing = jnp.take(block_table, picks, axis=0).reshape(wide_count, slot_cap, CBLK, width)
    fetched = lax.all_to_all(outgoing, "wide", split_axis=0, concat_axis=0, tiled=True)
    values = block_maxima(
        send_queries,
        fetched.reshape(slot_total, CBLK, width),
        jnp.arange(slot_total, dtype=jnp.int32),
    )
    per_request = jnp.take(values, req_pos, axis=0)
    best_score = jnp.max(per_request.reshape(query_count, K_CAND, QROWS), axis=1).reshape(emb_rows)
    return (new_centroids, best_score)


def solution(mesh):
    return jax.shard_map(
        local,
        mesh=mesh,
        in_specs=(
            P(("wide", "narrow"), None),
            P(("wide", "narrow"), None),
            P(("wide", "narrow")),
            P(("wide", "narrow"), None),
            P(("wide", "narrow"), None),
        ),
        out_specs=(P(("wide", "narrow"), None), P(("wide", "narrow"))),
        check_vma=False,
    )
```

profile of v0, /device:TPU:0, one launch (start us, length us, event | category | flops | bytes accessed | tf_op | source)
XLA Modules:
  0.0 827.5 jit_solution(12097914941548033054)
XLA Ops:
  7.2 0.7 fusion.22
  7.9 1.1 reduce-window.6
  9.0 0.2 slice_reduce_fusion
  9.2 0.8 fusion.19
  10.0 0.7 compare_select_fusion.2
  10.7 3.2 scatter_custom_fusion
  13.9 7.3 all-to-all-start
  21.2 3.6 scatter_custom_fusion.1
  24.7 2.8 all-to-all-done
  27.5 39.5 %all_to_all.28 = bf16[8,128,768]{2,1,0:T(8,128)(2,1)S(1)} all-to-all(bf16[8,128,768]{2,1,0:T(8,128)(2,1)S(1)} %bitcast.70), channel_id=1, replica_groups=mesh['wide'=8,'narrow'=4] {'wide'}, dimensions={0} | all-to-all | bytes 3145728 | tf_op jit(solution)/shard_map/all_to_all | solution.py:46
  67.0 5.9 fusion.16
  73.0 37.0 %reduce-scatter.2.cloned.1.call-done = bf16[512,768]{1,0:T(8,128)(2,1)} async-done(((bf16[2048,768]{1,0:T(8,128)(2,1)}), bf16[512,768]{1,0:T(8,128)(2,1)}) %reduce-scatter.2.cloned.1.call-update) | async-done | bytes 786448 | tf_op jit(solution)/shard_map/reduce_scatter | solution.py:61
  110.0 1.5 multiply_reduce_fusion
  111.5 2.3 multiply_convert_fusion
  113.8 0.1 reshape.273
  114.1 0.2 select_reduce_fusion
  114.3 0.7 scatter_custom_fusion.4
  115.1 11.8 %all_to_all.29 = s32[8,1,8]{2,1,0:T(1,128)S(1)} all-to-all(s32[8,1,8]{2,1,0:T(1,128)S(1)} %bitcast.76), channel_id=1, replica_groups=mesh['wide'=8,'narrow'=4] {'wide'}, dimensions={0} | all-to-all | bytes 512 | tf_op jit(solution)/shard_map/all_to_all | solution.py:93
  127.0 15.5 %all-gather.2.cloned.1.call-done = bf16[2048,768]{1,0:T(8,128)(2,1)} async-done(((bf16[512,768]{1,0:T(8,128)(2,1)}), bf16[2048,768]{1,0:T(8,128)(2,1)}) %all-gather.2.cloned.1.call-update) | async-done | bytes 3145744 | tf_op jit(solution)/shard_map/all_gather | solution.py:72
  142.5 12.2 %gather_fusion.2 = bf16[64,256,768]{2,1,0:T(8,128)(2,1)} fusion(bf16[8,256,768]{2,1,0:T(8,128)(2,1)} %bitcast.66, s32[1024]{0:T(1024)S(1)} %pad_clamp_fusion.2), kind=kCustom, calls=%fused_computation.2 | custom fusion | bytes 50331904 | tf_op jit(solution)/shard_map/jit(_take)/gather | solution.py:97
  154.7 21.3 %broadcast_select_fusion = bf16[8,8,256,768]{3,2,1,0:T(8,128)(2,1)} fusion(bf16[8,8,256,768]{3,2,1,0:T(8,128)(2,1)} %bitcast.68, pred[8,8]{1,0:T(8,128)(4,1)S(1)} %compare_and_fusion.1), kind=kLoop, calls=%fused_computation.25 | loop fusion | flops 12582912 | bytes 50331712 | tf_op jit(solution)/shard_map/jit(_take)/select_n | solution.py:97
  175.9 6.6 all-to-all-start.3
  182.6 0.7 scatter_custom_fusion.3
  183.3 0.1 broadcast_in_dim.109
  183.4 0.9 scatter_custom_fusion.2
  184.3 0.1 broadcast_in_dim.106
  184.4 6.9 gather_fusion.1
  191.3 11.1 %select_select_fusion = bf16[8,8,128,768]{3,2,1,0:T(8,128)(2,1)} fusion(bf16[8,8,128,768]{3,2,1,0:T(8,128)(2,1)} %bitcast.69, pred[8,8]{1,0:T(8,128)(4,1)S(1)} %broadcast_in_dim.109, pred[8,8]{1,0:T(8,128)(4,1)S(1)} %broadcast_in_dim.106), kind=kLoop, calls=%fused_computation.26 | loop fusion | flops 12582912 | bytes 25165952 | tf_op jit(solution)/shard_map/jit(_where)/select_n | solution.py:88
  202.5 523.3 %all-to-all-done.3 = bf16[8,8,256,768]{3,2,1,0:T(8,128)(2,1)} async-done(((bf16[8,8,256,768]{3,2,1,0:T(8,128)(2,1)}), bf16[8,8,256,768]{3,2,1,0:T(8,128)(2,1)}, u32[]{:S(2)}, u32[]{:S(2)}) %all-to-all-start.3) | async-done | bytes 25165856 | tf_op jit(solution)/shard_map/all_to_all | solution.py:98
  725.8 93.7 %while.10 = (s32[]{:T(128)}, f32[8,8,128]{2,1,0:T(8,128)S(1)}, bf16[8,8,128,768]{3,2,1,0:T(8,128)(2,1)}, s32[8,8]{1,0:T(8,128)S(1)}, bf16[64,256,768]{2,1,0:T(8,128)(2,1)}, /*index=5*/s32[]{:T(128)}) while((s32[]{:T(128)}, f32[8,8,128]{2,1,0:T(8,128)S(1)}, bf16[8,8,128,768]{3,2,1,0:T(8,128)(2,1)}, s32[8,8]{1,0:T(8,128)S(1)}, ...), condition=%wide.region_14.15_spmd, body=%wide.region_12.14_spmd.sunk | while | flops 404488256 | bytes 11027201 | solution.py:28
  725.8 8.9 %gather_fusion = bf16[8,256,768]{2,1,0:T(8,128)(2,1)S(1)} fusion(bf16[64,256,768]{2,1,0:T(8,128)(2,1)} %get-tuple-element.89, s32[1024]{0:T(1024)S(1)} %pad_clamp_fusion.5), kind=kCustom, calls=%fused_computation.clone.1 | custom fusion | bytes 6291488 | tf_op jit(solution)/shard_map/while/body/eval_jaxpr/jit(_take)/gather | solution.py:24
  734.7 2.7 fusion.45
  737.5 8.9 %gather_fusion = bf16[8,256,768]{2,1,0:T(8,128)(2,1)S(1)} fusion(bf16[64,256,768]{2,1,0:T(8,128)(2,1)} %get-tuple-element.89, s32[1024]{0:T(1024)S(1)} %pad_clamp_fusion.5), kind=kCustom, calls=%fused_computation.clone.1 | custom fusion | bytes 6291488 | tf_op jit(solution)/shard_map/while/body/eval_jaxpr/jit(_take)/gather | solution.py:24
  746.4 2.7 fusion.45
  749.2 8.9 %gather_fusion = bf16[8,256,768]{2,1,0:T(8,128)(2,1)S(1)} fusion(bf16[64,256,768]{2,1,0:T(8,128)(2,1)} %get-tuple-element.89, s32[1024]{0:T(1024)S(1)} %pad_clamp_fusion.5), kind=kCustom, calls=%fused_computation.clone.1 | custom fusion | bytes 6291488 | tf_op jit(solution)/shard_map/while/body/eval_jaxpr/jit(_take)/gather | solution.py:24
  758.1 2.7 fusion.45
  760.9 8.9 %gather_fusion = bf16[8,256,768]{2,1,0:T(8,128)(2,1)S(1)} fusion(bf16[64,256,768]{2,1,0:T(8,128)(2,1)} %get-tuple-element.89, s32[1024]{0:T(1024)S(1)} %pad_clamp_fusion.5), kind=kCustom, calls=%fused_computation.clone.1 | custom fusion | bytes 6291488 | tf_op jit(solution)/shard_map/while/body/eval_jaxpr/jit(_take)/gather | solution.py:24
  769.9 2.7 fusion.45
  772.6 8.9 %gather_fusion = bf16[8,256,768]{2,1,0:T(8,128)(2,1)S(1)} fusion(bf16[64,256,768]{2,1,0:T(8,128)(2,1)} %get-tuple-element.89, s32[1024]{0:T(1024)S(1)} %pad_clamp_fusion.5), kind=kCustom, calls=%fused_computation.clone.1 | custom fusion | bytes 6291488 | tf_op jit(solution)/shard_map/while/body/eval_jaxpr/jit(_take)/gather | solution.py:24
  781.6 2.7 fusion.45
  784.3 8.9 %gather_fusion = bf16[8,256,768]{2,1,0:T(8,128)(2,1)S(1)} fusion(bf16[64,256,768]{2,1,0:T(8,128)(2,1)} %get-tuple-element.89, s32[1024]{0:T(1024)S(1)} %pad_clamp_fusion.5), kind=kCustom, calls=%fused_computation.clone.1 | custom fusion | bytes 6291488 | tf_op jit(solution)/shard_map/while/body/eval_jaxpr/jit(_take)/gather | solution.py:24
  793.3 2.7 fusion.45
  796.1 8.9 %gather_fusion = bf16[8,256,768]{2,1,0:T(8,128)(2,1)S(1)} fusion(bf16[64,256,768]{2,1,0:T(8,128)(2,1)} %get-tuple-element.89, s32[1024]{0:T(1024)S(1)} %pad_clamp_fusion.5), kind=kCustom, calls=%fused_computation.clone.1 | custom fusion | bytes 6291488 | tf_op jit(solution)/shard_map/while/body/eval_jaxpr/jit(_take)/gather | solution.py:24
  805.0 2.7 fusion.45
  807.8 8.9 %gather_fusion = bf16[8,256,768]{2,1,0:T(8,128)(2,1)S(1)} fusion(bf16[64,256,768]{2,1,0:T(8,128)(2,1)} %get-tuple-element.89, s32[1024]{0:T(1024)S(1)} %pad_clamp_fusion.5), kind=kCustom, calls=%fused_computation.clone.1 | custom fusion | bytes 6291488 | tf_op jit(solution)/shard_map/while/body/eval_jaxpr/jit(_take)/gather | solution.py:24
  816.7 2.7 fusion.45
  819.5 0.6 gather_fusion.3
  820.0 0.7 fusion.20
  (67 shorter events, 1.0 us)
Async XLA Ops:
  13.9 13.6 %all-to-all-start = ((s32[8,1,128]{2,1,0:T(1,128)}), s32[8,1,128]{2,1,0:T(1,128)S(1)}, u32[]{:S(2)}, u32[]{:S(2)}) async-start(s32[8,1,128]{2,1,0:T(1,128)} %bitcast.11), calls=%async_computation | async-start | bytes 8192 | tf_op jit(solution)/shard_map/all_to_all | solution.py:53
  21.1 88.9 %reduce-scatter.2.cloned.1.call-start = ((), (), s32[]{:S(2)}) async-start(), calls=%async_computation.5 | async-start | bytes 3932160 | tf_op jit(solution)/shard_map/reduce_scatter | solution.py:61
  72.9 37.1 %copy-start.1 = (bf16[512,768]{1,0:T(8,128)(2,1)S(1)}, bf16[512,768]{1,0:T(8,128)(2,1)}, u32[]{:S(2)}) copy-start(bf16[512,768]{1,0:T(8,128)(2,1)} %param.10) | copy-start | bytes 2359300
  72.9 40.9 %copy-start.2 = (s32[4,8]{1,0:T(4,128)S(1)}, s32[4,8]{1,0:T(4,128)}, u32[]{:S(2)}) copy-start(s32[4,8]{1,0:T(4,128)} %param.11) | copy-start | bytes 388
  72.9 69.5 %all-gather.2.cloned.1.call-start = ((), (), s32[]{:S(2)}) async-start(), calls=%async_computation.6 | async-start | bytes 3932160 | tf_op jit(solution)/shard_map/all_gather | solution.py:72
  175.9 8.4 %copy-start = (bf16[512,768]{1,0:T(8,128)(2,1)S(1)}, bf16[512,768]{1,0:T(8,128)(2,1)}, u32[]{:S(2)}) copy-start(bf16[512,768]{1,0:T(8,128)(2,1)} %param.7) | copy-start | bytes 2359300
  175.9 549.8 %all-to-all-start.3 = ((bf16[8,8,256,768]{3,2,1,0:T(8,128)(2,1)}), bf16[8,8,256,768]{3,2,1,0:T(8,128)(2,1)}, u32[]{:S(2)}, u32[]{:S(2)}) async-start(bf16[8,8,256,768]{3,2,1,0:T(8,128)(2,1)} %broadcast_select_fusion), calls=%async_computation.4 | async-start | bytes 50331648 | tf_op jit(solution)/shard_map/all_to_all | solution.py:98
Sparse Core Ops, SparseCore 0:
  73.1 36.9 reduce-scatter.1
  113.9 28.5 all-gather.1
where the time goes:
time: 829 us; the launch traced here: 828 us
  waiting for transfers between devices  579 us (70%)
  local copies, waits for them, and re-layouts  101 us (12%)
  blocking collectives  51.2 us (6%)
  other arithmetic  40.8 us (5%)
  matrix products  27.6 us (3%)
  between operations  14.2 us (2%)
  starting transfers between devices  13.9 us (2%)
    all_to_all x1, waiting for transfers between devices, local(): lax.all_to_all(outgoing, 'wide', split_axis=0, concat_axis=0, tiled=True)  523 us
    gather x8, local copies, waits for them, and re-layouts, one_turn(): chosen = jnp.take(table, pick_part, axis=0)  71.2 us
    all_to_all x1, blocking collectives, local(): lax.all_to_all(send_rows.reshape(wide_count, row_cap, width), 'wide', spl...  39.5 us
    reduce_scatter x1, waiting for transfers between devices, local(): lax.psum_scatter(lax.dot_general(one_hot, flat_rows, (((0,), (0,)), ((),...  37 us
    dot_general x8, matrix products, one_turn(): jnp.einsum('gnd,gcd->gnc', query_part, chosen, preferred_element_type=jnp...  21.7 us
    select_n x2, other arithmetic, local(): jnp.take(block_table, picks, axis=0)  21.3 us
  transfers between devices with their start and end apart: 4, of which 4 were waited for; matrix products, arithmetic and copies ran while one was open for 3% of the time, Pallas kernels for 0%

commit v1 on v0

v1 whole, which is shorter than its diff:
```python
import functools

import jax
import jax.numpy as jnp
from jax import lax
from jax.experimental import pallas as pl
from jax.experimental.pallas import tpu as pltpu
from jax.sharding import PartitionSpec as P

QROWS = 128
CBLK = 256
K_CAND = 8
WORD = 32
MESH = pl.DeviceIdType.MESH


def refine_kernel(
    emb_ref, meta_ref, cent_ref, newc_ref, best_ref,
    emb_all, meta_all, cent_all, acc, psend, precv, newc, part, part_in,
    send_sem, recv_sem, meta_send, meta_recv, cent_sem, psum_send, psum_recv, part_send, part_recv,
):
    rows, width = emb_ref.shape
    half = rows // 2
    peers = emb_all.shape[0]
    chip_cents = cent_all.shape[0]
    tiles = chip_cents // CBLK
    wide = lax.axis_index("wide")
    narrow = lax.axis_index("narrow")
    z, x = wide // 2, wide % 2
    y, core = narrow // 2, narrow % 2
    me = wide * 2 + y
    low = z < 2
    inner = jnp.logical_or(z == 1, z == 2)
    outer = jnp.logical_not(inner)
    partner = z + 1 - 2 * (z % 2)
    across = 3 - z
    levels = (z, partner, jnp.where(low, 2, 1), jnp.where(low, 3, 0))

    def slot(column, k):
        xx = 1 - x if column in "XD" else x
        yy = 1 - y if column in "YD" else y
        return (levels[k] * 2 + xx) * 2 + yy

    slots = {c + str(k): slot(c, k) for c in "OXYD" for k in range(4)}

    def device(zz, xx, yy):
        return (zz * 2 + xx, yy * 2 + core)

    links = {
        "x": (0, device(z, 1 - x, y)),
        "y": (1, device(z, x, 1 - y)),
        "pair": (2, device(partner, x, y)),
        "cross": (3, device(across, x, y)),
    }
    twin = (wide, y * 2 + 1 - core)

    def peer(j):
        return (j // 2, (j % 2) * 2 + core)

    def chunk(link, j, h):
        number, target = links[link]
        piece = emb_all.at[j, pl.ds(h * half, half), :]
        return pltpu.make_async_remote_copy(
            src_ref=piece, dst_ref=piece, send_sem=send_sem.at[number, j, h],
            recv_sem=recv_sem.at[j, h], device_id=target, device_id_type=MESH,
        )

    sent = []

    def forward(name, h, *names):
        j = slots[name]
        for link in names:
            sent.append((link, j, h))
            if link == "cross":
                pl.when(inner)(lambda: chunk("cross", j, h).start())
            else:
                chunk(link, j, h).start()

    def forward_inner(name, h, link):
        j = slots[name]
        sent.append(("inner_" + link, j, h))
        chunk(link, j, h).start()

    def arrive(name, h):
        chunk("x", slots[name], h).wait_recv()

    barrier = pltpu.get_barrier_semaphore()

    @pl.loop(1, peers)
    def _(k):
        pl.semaphore_signal(barrier, inc=1, device_id=peer((me + k) % peers), device_id_type=MESH)

    pl.semaphore_signal(barrier, inc=1, device_id=twin, device_id_type=MESH)
    emb_all[me] = emb_ref[...]
    meta_all[me] = meta_ref[...]
    cent_all[pl.ds(pl.multiple_of(core * rows, rows), rows), :] = cent_ref[...]
    pl.semaphore_wait(barrier, peers)

    def meta_copy(target, source):
        return pltpu.make_async_remote_copy(
            src_ref=meta_ref, dst_ref=meta_all.at[source], send_sem=meta_send.at[target],
            recv_sem=meta_recv.at[source], device_id=peer(target), device_id_type=MESH,
        )

    def own_cents():
        return cent_all.at[pl.ds(pl.multiple_of(core * rows, rows), rows), :]

    cent_copy = pltpu.make_async_remote_copy(
        src_ref=own_cents(), dst_ref=own_cents(), send_sem=cent_sem.at[0],
        recv_sem=cent_sem.at[1], device_id=twin, device_id_type=MESH,
    )

    base = (wide * 4 + y * 2) * rows
    order = ("O0", "O1", "X0", "Y0", "X1", "Y1", "O2", "D0", "O3", "D1", "X2", "Y2", "D2", "X3", "Y3", "D3")

    def at_0():
        @pl.loop(1, peers)
        def _(k):
            meta_copy((me + k) % peers, me).start()

        for h in (0, 1):
            forward("O0", h, "pair", "cross", "x")
            forward("O0", 1 - h, "y")
        cent_copy.start()

        @pl.loop(1, peers)
        def _(k):
            j = (me + k) % peers
            meta_copy(j, j).wait_recv()

    def at_1():
        for h in (0, 1):
            arrive("O1", h)
            forward("O1", h, "cross", "x")
            if h == 1:
                forward("O1", 1, "y")
                forward("O1", 0, "y")

    def corner(k):
        def go():
            arrive(f"X{k}", 0)
            forward(f"X{k}", 0, "y")
            arrive(f"Y{k}", 1)
            forward(f"Y{k}", 1, "x")
            arrive(f"X{k}", 1)
            arrive(f"Y{k}", 0)

        return go

    def inner_to_pair(name):
        def go():
            @pl.when(inner)
            def _():
                for h in (0, 1):
                    arrive(name, h)
                    forward_inner(name, h, "pair")

        return go

    def outer_arrive(name):
        @pl.when(outer)
        def _():
            for h in (0, 1):
                arrive(name, h)

    def to_plane(name):
        def go():
            outer_arrive(name)
            for h in (0, 1):
                forward(name, h, "x")
                forward(name, 1 - h, "y")

        return go

    def to_cross(name):
        def go():
            for h in (0, 1):
                arrive(name, h)
                forward(name, h, "cross")

        return go

    def both(name):
        def go():
            for h in (0, 1):
                arrive(name, h)

        return go

    def at_10():
        inner_to_pair("D2")()
        both("X2")()

    def at_12():
        outer_arrive("D2")
        inner_to_pair("D3")()

    steps = (
        at_0, at_1, corner(0), inner_to_pair("O2"), corner(1), inner_to_pair("O3"),
        to_plane("O2"), to_cross("D0"), to_plane("O3"), to_cross("D1"),
        at_10, both("Y2"), at_12, both("X3"), both("Y3"), lambda: outer_arrive("D3"),
    )

    acc[...] = jnp.zeros_like(acc)

    @pl.loop(0, len(order))
    def _(i):
        j = jnp.int32(0)
        for n, step in enumerate(steps):
            pl.when(i == n)(step)
            j = j + jnp.where(i == n, slots[order[n]], 0)
        ids = meta_all[j][:, :rows] - base
        for t in range(tiles):
            spot = lax.broadcasted_iota(jnp.int32, (CBLK, rows), 0) + t * CBLK
            hot = jnp.where(spot == ids, 1.0, 0.0).astype(jnp.bfloat16)
            acc[t * CBLK : (t + 1) * CBLK, :] += jnp.dot(
                hot, emb_all[j], preferred_element_type=jnp.float32
            )

    def psum_copy(t):
        return pltpu.make_async_remote_copy(
            src_ref=psend.at[t], dst_ref=precv.at[t], send_sem=psum_send.at[t],
            recv_sem=psum_recv.at[t], device_id=twin, device_id_type=MESH,
        )

    for t in range(tiles):
        psend[t] = acc[t * CBLK : (t + 1) * CBLK, :].astype(jnp.bfloat16)
        psum_copy(t).start()
    cent_copy.wait()
    for t in range(tiles):
        psum_copy(t).wait()
        mixed = cent_all[t * CBLK : (t + 1) * CBLK, :].astype(jnp.float32) + (
            psend[t].astype(jnp.float32) + precv[t].astype(jnp.float32)
        )
        scale = lax.rsqrt(jnp.mean(mixed * mixed, axis=1, keepdims=True) + 1e-06)
        newc[t * CBLK : (t + 1) * CBLK, :] = (mixed * scale).astype(jnp.bfloat16)

    def part_copy(target, source):
        return pltpu.make_async_remote_copy(
            src_ref=part.at[target], dst_ref=part_in.at[source], send_sem=part_send.at[target],
            recv_sem=part_recv.at[source], device_id=peer(target), device_id_type=MESH,
        )

    first = (wide * 4 + y * 2) * (rows // CBLK)
    word, shift = first // WORD, first % WORD

    @pl.loop(1, peers + 1)
    def _(k):
        j = (me + k) % peers
        words = meta_all[j]
        bits = jnp.where(word == 0, words[:, rows : 2 * rows], words[:, 2 * rows : 3 * rows])
        best = jnp.full((1, rows), -jnp.inf, jnp.float32)
        for t in range(tiles):
            scores = lax.dot_general(
                newc[t * CBLK : (t + 1) * CBLK, :], emb_all[j], (((1,), (1,)), ((), ())),
                preferred_element_type=jnp.float32,
            )
            top = jnp.max(scores, axis=0, keepdims=True)
            live = jnp.bitwise_and(jnp.right_shift(bits, shift + t), 1) == 1
            best = jnp.maximum(best, jnp.where(live, top, -jnp.inf))
        part[j] = best

        @pl.when(k < peers)
        def _():
            part_copy(j, me).start()

    newc_ref[...] = newc[pl.ds(pl.multiple_of(core * rows, rows), rows), :]

    @pl.loop(1, peers)
    def _(k):
        j = (me + k) % peers
        part_copy(j, j).wait_recv()

    part_in[me] = part[me]
    best = part_in[0]
    for j in range(1, peers):
        best = jnp.maximum(best, part_in[j])
    best_ref[...] = best * width ** (-0.5)

    for link, j, h in sent:
        if link.startswith("inner_"):
            pl.when(inner)(lambda: chunk(link[6:], j, h).wait_send())
        elif link == "cross":
            pl.when(inner)(lambda: chunk(link, j, h).wait_send())
        else:
            chunk(link, j, h).wait_send()

    @pl.loop(1, peers)
    def _(k):
        j = (me + k) % peers
        meta_copy(j, me).wait_send()
        part_copy(j, me).wait_send()


def gathered_step(embeddings, coarse_ids, fine_ids, centroids, candidates):
    rows, width = embeddings.shape
    narrow_count = lax.axis_size("narrow")
    peers = lax.axis_size("wide") * narrow_count // 2
    assign = coarse_ids[:, 0] * (centroids.shape[0] * narrow_count) + fine_ids
    words = []
    for w in range(2):
        flags = jnp.where(
            candidates // WORD == w, jnp.left_shift(jnp.int32(1), candidates % WORD), 0
        )
        mask = flags[:, 0]
        for k in range(1, K_CAND):
            mask = jnp.bitwise_or(mask, flags[:, k])
        words.append(jnp.broadcast_to(mask[:, None], (mask.shape[0], QROWS)).reshape(rows))
    meta = jnp.concatenate([assign, *words]).reshape(1, 3 * rows)
    chip_cents = 2 * centroids.shape[0]
    tiles = chip_cents // CBLK
    new_centroids, best = pl.pallas_call(
        refine_kernel,
        out_shape=(
            jax.ShapeDtypeStruct(centroids.shape, jnp.bfloat16),
            jax.ShapeDtypeStruct((1, rows), jnp.float32),
        ),
        in_specs=[pl.BlockSpec(memory_space=pltpu.VMEM)] * 3,
        out_specs=(pl.BlockSpec(memory_space=pltpu.VMEM),) * 2,
        scratch_shapes=[
            pltpu.VMEM((peers, rows, width), jnp.bfloat16),
            pltpu.VMEM((peers, 1, 3 * rows), jnp.int32),
            pltpu.VMEM((chip_cents, width), jnp.bfloat16),
            pltpu.VMEM((chip_cents, width), jnp.float32),
            pltpu.VMEM((tiles, CBLK, width), jnp.bfloat16),
            pltpu.VMEM((tiles, CBLK, width), jnp.bfloat16),
            pltpu.VMEM((chip_cents, width), jnp.bfloat16),
            pltpu.VMEM((peers, 1, rows), jnp.float32),
            pltpu.VMEM((peers, 1, rows), jnp.float32),
            pltpu.SemaphoreType.DMA((4, peers, 2)),
            pltpu.SemaphoreType.DMA((peers, 2)),
            pltpu.SemaphoreType.DMA((peers,)),
            pltpu.SemaphoreType.DMA((peers,)),
            pltpu.SemaphoreType.DMA((2,)),
            pltpu.SemaphoreType.DMA((tiles,)),
            pltpu.SemaphoreType.DMA((tiles,)),
            pltpu.SemaphoreType.DMA((peers,)),
            pltpu.SemaphoreType.DMA((peers,)),
        ],
        compiler_params=pltpu.CompilerParams(
            collective_id=0, has_side_effects=True, vmem_limit_bytes=48 * 2**20
        ),
    )(embeddings, meta, centroids)
    return new_centroids, best.reshape(rows)


def slot_ranks(targets):
    place = jnp.arange(targets.shape[0], dtype=jnp.int32)
    same = targets[:, None] == targets[None, :]
    return jnp.sum((same & (place[None, :] < place[:, None])).astype(jnp.int32), axis=1)


def pick(table, index):
    return lax.map(lambda i: lax.dynamic_index_in_dim(table, i, keepdims=False), index)


def block_maxima(queries, blocks):
    def one(operands):
        query, block = operands
        scores = jnp.einsum("nd,cd->nc", query, block, preferred_element_type=jnp.float32)
        return jnp.max(scores, axis=1)

    return lax.map(one, (queries, blocks)) * queries.shape[2] ** (-0.5)


def routed_step(embeddings, coarse_ids, fine_ids, centroids, candidates):
    wide_count = lax.axis_size("wide")
    narrow_count = lax.axis_size("narrow")
    emb_rows, width = embeddings.shape
    cent_rows = centroids.shape[0]
    group_cents = cent_rows * narrow_count
    row_cap = (2 * emb_rows + wide_count - 1) // wide_count
    exchange = functools.partial(
        lax.all_to_all, axis_name="wide", split_axis=0, concat_axis=0, tiled=True
    )
    targets = coarse_ids[:, 0]
    row_pos = targets * row_cap + slot_ranks(targets)
    send_rows = jnp.zeros((wide_count * row_cap, width), jnp.bfloat16).at[row_pos].set(embeddings)
    send_fine = jnp.full((wide_count * row_cap,), -1, jnp.int32).at[row_pos].set(fine_ids)
    flat_rows = exchange(send_rows.reshape(wide_count, row_cap, width)).reshape(-1, width)
    flat_fine = exchange(send_fine.reshape(wide_count, row_cap)).reshape(-1)
    columns = jnp.arange(group_cents, dtype=jnp.int32)
    one_hot = (flat_fine[:, None] == columns[None, :]).astype(jnp.bfloat16)
    sums = lax.psum_scatter(
        lax.dot_general(
            one_hot, flat_rows, (((0,), (0,)), ((), ())), preferred_element_type=jnp.float32
        ).astype(jnp.bfloat16),
        "narrow",
        scatter_dimension=0,
        tiled=True,
    ).astype(jnp.float32)
    mixed = centroids.astype(jnp.float32) + sums
    scale_row = lax.rsqrt(jnp.mean(mixed * mixed, axis=1, keepdims=True) + 1e-06)
    new_centroids = (mixed * scale_row).astype(jnp.bfloat16)
    gathered = lax.all_gather(new_centroids, "narrow", axis=0, tiled=True)
    block_count = group_cents // CBLK
    block_table = gathered.reshape(block_count, CBLK, width)
    query_count = emb_rows // QROWS
    requests = query_count * K_CAND
    slot_cap = (2 * requests + wide_count - 1) // wide_count
    slot_total = wide_count * slot_cap
    wanted = candidates.reshape(-1)
    owner_group = wanted // block_count
    local_block = wanted - owner_group * block_count
    req_pos = owner_group * slot_cap + slot_ranks(owner_group)
    req_query = jnp.arange(requests, dtype=jnp.int32) // K_CAND
    slot_query = jnp.zeros((slot_total,), jnp.int32).at[req_pos].set(req_query)
    slot_block = jnp.full((slot_total,), -1, jnp.int32).at[req_pos].set(local_block)
    query_blocks = embeddings.reshape(query_count, QROWS, width)
    ids_in = exchange(slot_block.reshape(wide_count, slot_cap))
    picks = jnp.clip(ids_in.reshape(-1), 0, block_count - 1)
    outgoing = pick(block_table, picks).reshape(wide_count, slot_cap, CBLK, width)
    fetched = exchange(outgoing).reshape(slot_total, CBLK, width)
    values = block_maxima(pick(query_blocks, slot_query), fetched)
    per_request = pick(values, req_pos)
    best_score = jnp.max(per_request.reshape(query_count, K_CAND, QROWS), axis=1).reshape(emb_rows)
    return (new_centroids, best_score)


def solution(mesh):
    gathered = mesh.shape["wide"] == 8 and mesh.shape["narrow"] == 4
    return jax.shard_map(
        gathered_step if gathered else routed_step,
        mesh=mesh,
        in_specs=(
            P(("wide", "narrow"), None),
            P(("wide", "narrow"), None),
            P(("wide", "narrow")),
            P(("wide", "narrow"), None),
            P(("wide", "narrow"), None),
        ),
        out_specs=(P(("wide", "narrow"), None), P(("wide", "narrow"))),
        check_vma=False,
    )
```

time: 829 us -> 128 us (0.15)
  waiting for transfers between devices: 579 us -> 0 us
  Pallas kernels: 0 us -> 122 us
  local copies, waits for them, and re-layouts: 101 us -> 4.55 us
  blocking collectives: 51.2 us -> 0 us
  other arithmetic: 40.8 us -> 0.91 us
  matrix products: 27.6 us -> 0 us
  starting transfers between devices: 13.9 us -> 0 us
  between operations: 14.2 us -> 0.67 us
    all_to_all x2 -> x0, waiting for transfers between devices: 526 us -> none  [the longest x1 523 us: local(): lax.all_to_all(outgoing, 'wide', split_axis=0, concat_axis=0, tiled=True)]
    pallas_call x0 -> x1, Pallas kernels: none -> 122 us  [gathered_step(): pl.pallas_call(refine_kernel, out_shape=(jax.ShapeDtypeStruct(centroids.s...]
    gather x11 -> x0, local copies, waits for them, and re-layouts: 90.9 us -> none  [the longest x8 71.2 us: one_turn(): chosen = jnp.take(table, pick_part, axis=0)]
    all_to_all x2 -> x0, blocking collectives: 51.2 us -> none  [the longest x1 39.5 us: local(): lax.all_to_all(send_rows.reshape(wide_count, row_cap, width), 'wide', spl...]
    reduce_scatter x1 -> x0, waiting for transfers between devices: 37 us -> none  [local(): lax.psum_scatter(lax.dot_general(one_hot, flat_rows, (((0,), (0,)), ((),...]
    select_n x15 -> x1, other arithmetic: 33.2 us -> 0.01 us  [gathered_step(): jnp.where(candidates // WORD == w, jnp.left_shift(jnp.int32(1), candidate...]
    dot_general x9 -> x0, matrix products: 27.6 us -> none  [the longest x8 21.7 us: one_turn(): jnp.einsum('gnd,gcd->gnc', query_part, chosen, preferred_element_type=jnp...]
    all_gather x1 -> x0, waiting for transfers between devices: 15.5 us -> none  [local(): gathered = lax.all_gather(new_centroids, 'narrow', axis=0, tiled=True)]
  transfers between devices with their start and end apart: 4 -> 0, of which waited for: 4 -> 0; matrix products, arithmetic and copies ran while one was open for 3% -> 0% of each run, Pallas kernels for 0% -> 0%
where the time goes in v1:
time: 128 us
  Pallas kernels  122 us (95%)
  local copies, waits for them, and re-layouts  4.55 us (4%)
    pallas_call x1, Pallas kernels, gathered_step(): pl.pallas_call(refine_kernel, out_shape=(jax.ShapeDtypeStruct(centroids.s...  122 us
    unnamed x10, local copies, waits for them, and re-layouts  4.4 us

profile of v1, /device:TPU:0, one launch (start us, length us, event | category | flops | bytes accessed | tf_op | source)
XLA Modules:
  0.0 128.2 jit_solution(5724910225777947083)
XLA Ops:
  0.6 0.0 copy-start.2
  0.6 0.7 broadcast_multiply_fusion
  1.3 0.0 copy-done.2
  1.3 0.0 copy-start.3
  1.3 0.7 copy-done.3
  2.0 0.2 or_reduce_fusion
  2.2 0.1 broadcast_bitcast_fusion
  2.3 0.1 broadcast_bitcast_fusion.1
  2.4 0.0 copy-start
  2.4 1.1 copy-done
  3.5 0.0 copy-start.1
  3.5 1.1 copy-done.1
  4.7 122.0 %shard_map.68 = (bf16[512,768]{1,0:T(8,128)(2,1)S(1)}, f32[1,512]{1,0:T(1,128)S(1)}) custom-call(bf16[512,768]{1,0:T(8,128)(2,1)S(1)} %copy-done, s32[1,1536]{1,0:T(1,128)S(1)} %reshape.20.meta_ref, bf16[512,768]{1,0:T(8,128)(2,1)S(1)} %copy-done.1), custom_call_target="tpu_custom_call" | custom-call | tf_op jit(solution)/shard_map/pallas_call | solution.py:312
  126.7 0.9 copy.9
  127.6 0.6 copy.10
  (4 shorter events, 0.0 us)
Async XLA Ops:
  0.6 0.7 copy-start.2
  1.3 0.7 copy-start.3
  2.4 1.1 copy-start
  3.5 1.1 copy-start.1

commit v2 on v1

--- a/solution.py
+++ b/solution.py
@@ -16,7 +16,7 @@
 
 def refine_kernel(
     emb_ref, meta_ref, cent_ref, newc_ref, best_ref,
-    emb_all, meta_all, cent_all, acc, psend, precv, newc, part, part_in,
+    emb_all, meta_all, cent_all, acc, psend, precv, newc, part, part_in, load_sem,
     send_sem, recv_sem, meta_send, meta_recv, cent_sem, psum_send, psum_recv, part_send, part_recv,
 ):
     rows, width = emb_ref.shape
@@ -84,6 +84,14 @@
     def arrive(name, h):
         chunk("x", slots[name], h).wait_recv()
 
+    def own_cents():
+        return cent_all.at[pl.ds(pl.multiple_of(core * rows, rows), rows), :]
+
+    emb_load = pltpu.make_async_copy(emb_ref, emb_all.at[me], load_sem.at[0])
+    cent_load = pltpu.make_async_copy(cent_ref, own_cents(), load_sem.at[1])
+    emb_load.start()
+    cent_load.start()
+
     barrier = pltpu.get_barrier_semaphore()
 
     @pl.loop(1, peers)
@@ -91,9 +99,10 @@
         pl.semaphore_signal(barrier, inc=1, device_id=peer((me + k) % peers), device_id_type=MESH)
 
     pl.semaphore_signal(barrier, inc=1, device_id=twin, device_id_type=MESH)
-    emb_all[me] = emb_ref[...]
     meta_all[me] = meta_ref[...]
-    cent_all[pl.ds(pl.multiple_of(core * rows, rows), rows), :] = cent_ref[...]
+    acc[...] = jnp.zeros_like(acc)
+    emb_load.wait()
+    cent_load.wait()
     pl.semaphore_wait(barrier, peers)
 
     def meta_copy(target, source):
@@ -102,18 +111,13 @@
             recv_sem=meta_recv.at[source], device_id=peer(target), device_id_type=MESH,
         )
 
-    def own_cents():
-        return cent_all.at[pl.ds(pl.multiple_of(core * rows, rows), rows), :]
-
     cent_copy = pltpu.make_async_remote_copy(
         src_ref=own_cents(), dst_ref=own_cents(), send_sem=cent_sem.at[0],
         recv_sem=cent_sem.at[1], device_id=twin, device_id_type=MESH,
     )
 
     base = (wide * 4 + y * 2) * rows
-    order = ("O0", "O1", "X0", "Y0", "X1", "Y1", "O2", "D0", "O3", "D1", "X2", "Y2", "D2", "X3", "Y3", "D3")
-
-    def at_0():
+    def start():
         @pl.loop(1, peers)
         def _(k):
             meta_copy((me + k) % peers, me).start()
@@ -123,55 +127,42 @@
             forward("O0", 1 - h, "y")
         cent_copy.start()
 
+    def metas():
         @pl.loop(1, peers)
         def _(k):
             j = (me + k) % peers
             meta_copy(j, j).wait_recv()
 
-    def at_1():
-        for h in (0, 1):
-            arrive("O1", h)
-            forward("O1", h, "cross", "x")
-            if h == 1:
-                forward("O1", 1, "y")
-                forward("O1", 0, "y")
-
     def corner(k):
         def go():
             arrive(f"X{k}", 0)
             forward(f"X{k}", 0, "y")
             arrive(f"Y{k}", 1)
             forward(f"Y{k}", 1, "x")
-            arrive(f"X{k}", 1)
-            arrive(f"Y{k}", 0)
-
-        return go
-
-    def inner_to_pair(name):
-        def go():
-            @pl.when(inner)
-            def _():
-                for h in (0, 1):
-                    arrive(name, h)
-                    forward_inner(name, h, "pair")
-
-        return go
-
-    def outer_arrive(name):
-        @pl.when(outer)
-        def _():
-            for h in (0, 1):
-                arrive(name, h)
+
+        return go
 
     def to_plane(name):
         def go():
-            outer_arrive(name)
             for h in (0, 1):
                 forward(name, h, "x")
                 forward(name, 1 - h, "y")
 
         return go
 
+    def wait(name, *halves):
+        def go():
+            for h in halves:
+                arrive(name, h)
+
+        return go
+
+    def wait_outer(name, *halves):
+        def go():
+            pl.when(outer)(wait(name, *halves))
+
+        return go
+
     def to_cross(name):
         def go():
             for h in (0, 1):
@@ -180,41 +171,71 @@
 
         return go
 
-    def both(name):
-        def go():
-            for h in (0, 1):
-                arrive(name, h)
-
-        return go
-
-    def at_10():
-        inner_to_pair("D2")()
-        both("X2")()
-
-    def at_12():
-        outer_arrive("D2")
-        inner_to_pair("D3")()
+    def to_pair(name, *halves):
+        def go():
+            @pl.when(inner)
+            def _():
+                for h in halves:
+                    arrive(name, h)
+                    forward_inner(name, h, "pair")
+
+        return go
 
     steps = (
-        at_0, at_1, corner(0), inner_to_pair("O2"), corner(1), inner_to_pair("O3"),
-        to_plane("O2"), to_cross("D0"), to_plane("O3"), to_cross("D1"),
-        at_10, both("Y2"), at_12, both("X3"), both("Y3"), lambda: outer_arrive("D3"),
+        ("O0", 0, start),
+        ("O0", 1),
+        ("X0", 0, corner(0), metas),
+        ("Y0", 1),
+        ("O1", 0, to_cross("O1"), to_pair("O2", 0, 1), to_plane("O1")),
+        ("O1", 1),
+        ("X0", 1, wait("X0", 1)),
+        ("Y0", 0, wait("Y0", 0)),
+        ("D0", 0, to_cross("D0")),
+        ("D0", 1),
+        ("X1", 0, to_pair("O3", 0, 1), corner(1)),
+        ("Y1", 1),
+        ("O2", 0, wait_outer("O2", 0, 1), to_plane("O2")),
+        ("O2", 1),
+        ("X1", 1, wait("X1", 1)),
+        ("Y1", 0, wait("Y1", 0)),
+        ("D1", 0, to_pair("D2", 0, 1), to_cross("D1")),
+        ("D1", 1),
+        ("O3", 0, wait_outer("O3", 0, 1), to_plane("O3")),
+        ("O3", 1),
+        ("X2", 0, wait("X2", 0)),
+        ("Y2", 1, to_pair("D3", 0), wait("Y2", 1)),
+        ("X2", 1, to_pair("D3", 1), wait("X2", 1)),
+        ("Y2", 0, wait("Y2", 0)),
+        ("D2", 0, wait_outer("D2", 0)),
+        ("D2", 1, wait_outer("D2", 1)),
+        ("X3", 0, wait("X3", 0)),
+        ("Y3", 1, wait("Y3", 1)),
+        ("D3", 0, wait_outer("D3", 0)),
+        ("X3", 1, wait("X3", 1)),
+        ("Y3", 0, wait("Y3", 0)),
+        ("D3", 1, wait_outer("D3", 1)),
     )
 
-    acc[...] = jnp.zeros_like(acc)
-
-    @pl.loop(0, len(order))
+    @pl.loop(0, len(steps))
     def _(i):
-        j = jnp.int32(0)
-        for n, step in enumerate(steps):
-            pl.when(i == n)(step)
-            j = j + jnp.where(i == n, slots[order[n]], 0)
-        ids = meta_all[j][:, :rows] - base
+        j, h = jnp.int32(0), jnp.int32(0)
+        for n, (name, which, *events) in enumerate(steps):
+            if events:
+
+                @pl.when(i == n)
+                def _():
+                    for event in events:
+                        event()
+
+            j = j + jnp.where(i == n, slots[name], 0)
+            h = h + jnp.where(i == n, which, 0)
+        piece = pl.ds(pl.multiple_of(h * half, half), half)
+        ids = meta_all[j, :, piece] - base
         for t in range(tiles):
-            spot = lax.broadcasted_iota(jnp.int32, (CBLK, rows), 0) + t * CBLK
+            spot = lax.broadcasted_iota(jnp.int32, (CBLK, half), 0) + t * CBLK
             hot = jnp.where(spot == ids, 1.0, 0.0).astype(jnp.bfloat16)
             acc[t * CBLK : (t + 1) * CBLK, :] += jnp.dot(
-                hot, emb_all[j], preferred_element_type=jnp.float32
+                hot, emb_all[j, piece, :], preferred_element_type=jnp.float32
             )
 
     def psum_copy(t):
@@ -227,7 +248,8 @@
         psend[t] = acc[t * CBLK : (t + 1) * CBLK, :].astype(jnp.bfloat16)
         psum_copy(t).start()
     cent_copy.wait()
-    for t in range(tiles):
+
+    def normalise(t):
         psum_copy(t).wait()
         mixed = cent_all[t * CBLK : (t + 1) * CBLK, :].astype(jnp.float32) + (
             psend[t].astype(jnp.float32) + precv[t].astype(jnp.float32)
@@ -243,6 +265,9 @@
 
     first = (wide * 4 + y * 2) * (rows // CBLK)
     word, shift = first // WORD, first % WORD
+
+    for t in range(tiles):
+        normalise(t)
 
     @pl.loop(1, peers + 1)
     def _(k):
@@ -315,7 +340,11 @@
             jax.ShapeDtypeStruct(centroids.shape, jnp.bfloat16),
             jax.ShapeDtypeStruct((1, rows), jnp.float32),
         ),
-        in_specs=[pl.BlockSpec(memory_space=pltpu.VMEM)] * 3,
+        in_specs=[
+            pl.BlockSpec(memory_space=pltpu.HBM),
+            pl.BlockSpec(memory_space=pltpu.VMEM),
+            pl.BlockSpec(memory_space=pltpu.HBM),
+        ],
         out_specs=(pl.BlockSpec(memory_space=pltpu.VMEM),) * 2,
         scratch_shapes=[
             pltpu.VMEM((peers, rows, width), jnp.bfloat16),
@@ -327,6 +356,7 @@
             pltpu.VMEM((chip_cents, width), jnp.bfloat16),
             pltpu.VMEM((peers, 1, rows), jnp.float32),
             pltpu.VMEM((peers, 1, rows), jnp.float32),
+            pltpu.SemaphoreType.DMA((2,)),
             pltpu.SemaphoreType.DMA((4, peers, 2)),
             pltpu.SemaphoreType.DMA((peers, 2)),
             pltpu.SemaphoreType.DMA((peers,)),

time: 128 us -> 126 us (0.984)
  Pallas kernels: 122 us -> 119 us
    pallas_call x1, Pallas kernels: 122 us -> 119 us  [gathered_step(): pl.pallas_call(refine_kernel, out_shape=(jax.ShapeDtypeStruct(centroids.s...]
where the time goes in v2:
time: 126 us; the launch traced here: 125 us
  Pallas kernels  119 us (94%)
  local copies, waits for them, and re-layouts  4.55 us (4%)
    pallas_call x1, Pallas kernels, gathered_step(): pl.pallas_call(refine_kernel, out_shape=(jax.ShapeDtypeStruct(centroids.s...  119 us
    unnamed x10, local copies, waits for them, and re-layouts  4.4 us

profile of v2, /device:TPU:0, one launch (start us, length us, event | category | flops | bytes accessed | tf_op | source)
XLA Modules:
  0.0 125.3 jit_solution(11013710196866934665)
XLA Ops:
  0.6 0.0 copy-start.2
  0.6 0.7 broadcast_multiply_fusion
  1.3 0.0 copy-done.2
  1.3 0.0 copy-start.3
  1.3 0.7 copy-done.3
  2.0 0.2 or_reduce_fusion
  2.2 0.1 broadcast_bitcast_fusion
  2.3 0.1 broadcast_bitcast_fusion.1
  2.4 0.0 copy-start
  2.4 1.1 copy-done
  3.5 0.0 copy-start.1
  3.5 1.1 copy-done.1
  4.7 119.2 %shard_map.68 = (bf16[512,768]{1,0:T(8,128)(2,1)S(1)}, f32[1,512]{1,0:T(1,128)S(1)}) custom-call(bf16[512,768]{1,0:T(8,128)(2,1)S(1)} %copy-done, s32[1,1536]{1,0:T(1,128)S(1)} %reshape.20.meta_ref, bf16[512,768]{1,0:T(8,128)(2,1)S(1)} %copy-done.1), custom_call_target="tpu_custom_call" | custom-call | tf_op jit(solution)/shard_map/pallas_call | solution.py:337
  123.8 0.9 copy.9
  124.7 0.6 copy.10
  (4 shorter events, 0.0 us)
Async XLA Ops:
  0.6 0.7 copy-start.2
  1.3 0.7 copy-start.3
  2.4 1.1 copy-start
  3.5 1.1 copy-start.1
